TPU v7x, 32 devices: a whole 2x2x4 slice. The times are simulated.
32 devices in a mesh: dp: 16 (over z, y, core), ctx: 2 (over x).
Axes of the slice: x: 2, y: 2, z: 4, core: 2. Of those that a mesh axis runs over, the one named last changes fastest.
Arguments:
- frames: bfloat16 [16, 1024, 1280], P('dp', 'ctx'), may hold values from -6 to 6
- conv_taps: float32 [31, 1280], replicated, may hold values from -1 to 1
- conv_gain: float32 [1280], replicated, may hold values from 0.1 to 1.9
- w_kv: bfloat16 [1280, 2560], P('dp'), may hold values from -0.15625 to 0.15625
- queries: bfloat16 [16, 32, 1280], P('dp', 'ctx'), may hold values from -6 to 6
- out_grad: bfloat16 [16, 32, 1280], P('dp', 'ctx'), may hold values from -6 to 6
- frame_len: int32 [16], P('dp'), may hold values from 256 to 1024
- token_len: int32 [16], P('dp'), may hold values from 8 to 32
Outputs:
- frames_grad: bfloat16 [16, 1024, 1280], P('dp', 'ctx')
- taps_grad: float32 [31, 1280], replicated
- gain_grad: float32 [1280], replicated
- w_kv_grad: float32 [1280, 2560], P('dp')
- queries_grad: bfloat16 [16, 32, 1280], P('dp', 'ctx')
Inputs may be any that keep to these rules, and one draw needn't show every extreme that they name: frames at positions of frame_len[b] or beyond are padding of utterance b. Tokens at positions of token_len[b] or beyond are padding of utterance b.
All inputs are finite; a program needn't handle non-finite values.
Results may differ from a plain program's by a relative error of at most 0.012.
Values may be sent and summed in bfloat16 or wider, within the bound.
A program may use at most 128 MiB of HBM per device.

v0:
```python
import jax
import jax.numpy as jnp
from jax import lax
from jax.sharding import PartitionSpec as P

HEADS = 20


def padded_2(block, sides, width):
    for axis, dim in sides:
        count = lax.axis_size(axis)
        forward = [(i, i + 1) for i in range(count - 1)]
        backward = [(target, source) for source, target in forward]
        low = lax.ppermute(
            lax.slice_in_dim(block, block.shape[dim] - width, None, axis=dim), axis, forward
        )
        high = lax.ppermute(lax.slice_in_dim(block, 0, width, axis=dim), axis, backward)
        block = jnp.concatenate([low, block, high], axis=dim)
    return block


def shifted(value, axis, steps):
    count = lax.axis_size(axis)
    pairs = [(source, (source + steps) % count) for source in range(count)]
    return lax.ppermute(value, axis, pairs)


def conv_time(padded, conv_taps, length):
    total = jnp.zeros((length, padded.shape[1]), jnp.float32)
    for tap_idx in range(conv_taps.shape[0]):
        total = total + conv_taps[tap_idx] * padded[tap_idx : tap_idx + length].astype(jnp.float32)
    return total


def silu_slope(gated):
    sigma = jax.nn.sigmoid(gated)
    return sigma * (1.0 + gated * (1.0 - sigma))


def forward_part(query_block, key_block, value_block, live_mask, head_count):
    row_count = query_block.shape[0]
    frame_count = key_block.shape[0]
    q_heads = query_block.reshape(row_count, head_count, -1)
    k_heads = key_block.reshape(frame_count, head_count, -1)
    v_heads = value_block.reshape(frame_count, head_count, -1)
    scale = q_heads.shape[2] ** (-0.5)
    exp_scores = (
        jnp.exp(
            jnp.einsum("thd,fhd->htf", q_heads, k_heads, preferred_element_type=jnp.float32) * scale
        )
        * live_mask
    )
    totals = jnp.sum(exp_scores, axis=2).T
    weighted = jnp.einsum(
        "htf,fhd->thd", exp_scores.astype(jnp.bfloat16), v_heads, preferred_element_type=jnp.float32
    )
    return (weighted.reshape(row_count, -1), totals)


def backward_part(
    query_block, grad_block, totals, delta_rows, key_block, value_block, live_mask, head_count
):
    row_count = query_block.shape[0]
    frame_count = key_block.shape[0]
    q_heads = query_block.reshape(row_count, head_count, -1)
    g_heads = grad_block.reshape(row_count, head_count, -1)
    k_heads = key_block.reshape(frame_count, head_count, -1)
    v_heads = value_block.reshape(frame_count, head_count, -1)
    scale = q_heads.shape[2] ** (-0.5)
    exp_scores = (
        jnp.exp(
            jnp.einsum("thd,fhd->htf", q_heads, k_heads, preferred_element_type=jnp.float32) * scale
        )
        * live_mask
    )
    attn_prob = exp_scores / totals.T[:, :, None]
    d_prob = jnp.einsum("thd,fhd->htf", g_heads, v_heads, preferred_element_type=jnp.float32)
    d_score = (attn_prob * (d_prob - delta_rows.T[:, :, None])).astype(jnp.bfloat16)
    query_part = jnp.einsum(
        "htf,fhd->thd", d_score, k_heads, preferred_element_type=jnp.float32
    ).reshape(row_count, -1)
    key_part = jnp.einsum(
        "htf,thd->fhd", d_score, q_heads, preferred_element_type=jnp.float32
    ).reshape(frame_count, -1)
    value_part = jnp.einsum(
        "htf,thd->fhd", attn_prob.astype(jnp.bfloat16), g_heads, preferred_element_type=jnp.float32
    ).reshape(frame_count, -1)
    return (query_part, key_part, value_part)


def row_delta(weighted, totals, grad_block):
    row_count = weighted.shape[0]
    head_count = totals.shape[1]
    head_dim = weighted.shape[1] // head_count
    attended = weighted / jnp.repeat(totals, head_dim, axis=1)
    return jnp.sum(
        (grad_block.astype(jnp.float32) * attended).reshape(row_count, head_count, head_dim), axis=2
    )


def per_device(frames, conv_taps, conv_gain, w_kv, queries, out_grad, frame_len, token_len):
    cycle_size = lax.axis_size("ctx")
    cycle_pos = lax.axis_index("ctx")
    length = frames.shape[1]
    model_width = frames.shape[2]
    tokens = queries.shape[1]
    tap_count = conv_taps.shape[0]
    rim_width = tap_count // 2
    scale = (model_width // HEADS) ** (-0.5)
    padded = padded_2(frames, (("ctx", 1),), rim_width)[0]
    conv_out = conv_time(padded, conv_taps, length)
    gated = conv_gain * conv_out
    encoded = (frames[0].astype(jnp.float32) + jax.nn.silu(gated)).astype(jnp.bfloat16)
    w_full = lax.all_gather(w_kv, "dp", axis=0, tiled=True)
    key_values = jnp.dot(encoded, w_full, preferred_element_type=jnp.float32).astype(jnp.bfloat16)
    key_block = key_values[:, :model_width]
    value_block = key_values[:, model_width:]
    frame_pos = cycle_pos * length + jnp.arange(length)
    live_mask = (frame_pos < frame_len[0]).astype(jnp.float32)
    token_pos = cycle_pos * tokens + jnp.arange(tokens)
    grad_block = out_grad[0] * (token_pos < token_len[0]).astype(jnp.bfloat16)[:, None]
    query_block = queries[0]

    def forward_tile(visitor, keys_part, values_part, head_count):
        return forward_part(visitor, keys_part, values_part, live_mask, head_count)

    def backward_tile(
        visitor, visit_grad, visit_totals, visit_delta, keys_part, values_part, head_count
    ):
        return backward_part(
            visitor,
            visit_grad,
            visit_totals,
            visit_delta,
            keys_part,
            values_part,
            live_mask,
            head_count,
        )

    def forward_turn(turn_idx, carried):
        visitor, weighted, totals = carried
        part_sum, part_total = forward_tile(visitor, key_block, value_block, HEADS)
        visitor = shifted(visitor, "ctx", 1)
        weighted, totals = shifted((weighted + part_sum, totals + part_total), "ctx", 1)
        return (visitor, weighted, totals)

    first_state = (
        query_block,
        jnp.zeros((tokens, model_width), jnp.float32),
        jnp.zeros((tokens, HEADS), jnp.float32),
    )
    first_out = lax.fori_loop(0, cycle_size, forward_turn, first_state)
    totals = first_out[2]
    delta_rows = row_delta(first_out[1], totals, grad_block)

    def backward_turn(turn_idx, carried):
        visitor, visit_grad, visit_totals, visit_delta, query_acc, key_acc, value_acc = carried
        part_query, part_key, part_value = backward_tile(
            visitor, visit_grad, visit_totals, visit_delta, key_block, value_block, HEADS
        )
        visitor, visit_grad = shifted((visitor, visit_grad), "ctx", 1)
        visit_totals, visit_delta, query_acc = shifted(
            (visit_totals, visit_delta, query_acc + part_query), "ctx", 1
        )
        return (
            visitor,
            visit_grad,
            visit_totals,
            visit_delta,
            query_acc,
            key_acc + part_key,
            value_acc + part_value,
        )

    second_state = (
        query_block,
        grad_block,
        totals,
        delta_rows,
        jnp.zeros((tokens, model_width), jnp.float32),
        jnp.zeros((length, model_width), jnp.float32),
        jnp.zeros((length, model_width), jnp.float32),
    )
    second_out = lax.fori_loop(0, cycle_size, backward_turn, second_state)
    query_acc = second_out[4]
    key_acc = second_out[5]
    value_acc = second_out[6]
    queries_grad = (query_acc * scale).astype(jnp.bfloat16)[None]
    kv_grad = jnp.concatenate([key_acc * scale, value_acc], 1).astype(jnp.bfloat16)
    enc_grad = lax.dot_general(
        kv_grad, w_full, (((1,), (1,)), ((), ())), preferred_element_type=jnp.float32
    )
    gated_grad = enc_grad * silu_slope(gated)
    gain_term = jnp.sum(gated_grad * conv_out, axis=0)
    conv_grad = gated_grad * conv_gain
    tap_terms = jnp.stack(
        [
            jnp.sum(conv_grad * padded[tap_idx : tap_idx + length].astype(jnp.float32), axis=0)
            for tap_idx in range(tap_count)
        ]
    )
    padded_grad = padded_2(conv_grad[None], (("ctx", 1),), rim_width)[0]
    back_conv = jnp.zeros((length, model_width), jnp.float32)
    for tap_idx in range(tap_count):
        offset = 2 * rim_width - tap_idx
        back_conv = back_conv + conv_taps[tap_idx] * padded_grad[offset : offset + length]
    frames_grad = (enc_grad + back_conv).astype(jnp.bfloat16)[None]
    taps_grad, gain_grad = lax.psum((tap_terms, gain_term), ("dp", "ctx"))
    data_part = lax.psum_scatter(
        lax.dot_general(
            encoded, kv_grad, (((0,), (0,)), ((), ())), preferred_element_type=jnp.float32
        ),
        "dp",
        scatter_dimension=0,
        tiled=True,
    )
    w_kv_grad = lax.psum(data_part, "ctx")
    return (frames_grad, taps_grad, gain_grad, w_kv_grad, queries_grad)


def solution(mesh):
    placed = (
        P("dp", "ctx", None),
        P(),
        P(),
        P("dp", None),
        P("dp", "ctx", None),
        P("dp", "ctx", None),
        P("dp"),
        P("dp"),
    )
    return jax.shard_map(
        per_device,
        mesh=mesh,
        in_specs=placed,
        out_specs=(P("dp", "ctx", None), P(), P(), P("dp", None), P("dp", "ctx", None)),
        check_vma=False,
    )
```

profile of v0, /device:TPU:0, one launch (start us, length us, event | category | flops | bytes accessed | tf_op | source)
XLA Modules:
  0.0 496.1 jit_solution(5663490250576671858)
XLA Ops:
  7.2 1.5 copy.116
  9.6 4.8 collective-permute-start.8
  18.0 1.8 slice_reduce_fusion.30
  19.9 1.5 constant_dynamic-update-slice_fusion.1
  22.3 12.4 %fusion.82 = (bf16[512,1280]{1,0:T(8,128)(2,1)}, f32[512,1280]{1,0:T(8,128)}) fusion(bf16[1,512,1280]{2,1,0:T(8,128)(2,1)S(1)} %copy-done.4, f32[1280]{0:T(1024)S(1)} %copy-done.75, bf16[1,527,1280]{2,1,0:T(8,128)(2,1)S(1)} %constant_dynamic-update-slice_fusion, f32[1280]{0:T(1024)S(1)} %get-tuple-element.290, f32[1280]{0:T(1024)S(1)} %get-tuple-element.291, ...), kind=kLoop, calls=%fused_computation.196 | loop fusion | flops 104202240 | bytes 25105920 | tf_op jit(solution)/shard_map/convert_element_type | solution.py:113
  35.0 41.4 %all-gather.2.cloned.1.call-done = bf16[1280,2560]{1,0:T(8,128)(2,1)} async-done(((bf16[80,2560]{1,0:T(8,128)(2,1)}), bf16[1280,2560]{1,0:T(8,128)(2,1)}) %all-gather.2.cloned.1.call-update) | async-done | bytes 6553616 | tf_op jit(solution)/shard_map/all_gather | solution.py:114
  76.4 6.8 %convolution_convert_fusion = bf16[512,2560]{1,0:T(8,128)(2,1)S(1)} fusion(bf16[512,1280]{1,0:T(8,128)(2,1)} %get-tuple-element.335, bf16[1280,2560]{1,0:T(8,128)(2,1)} %all-gather.2.cloned.1.call-done), kind=kOutput, calls=%fused_computation.72 | convolution fusion | flops 3356753920 | bytes 10485760 | tf_op jit(solution)/shard_map/dot_general | solution.py:115
  83.3 1.7 fusion.242
  85.0 1.6 copy.43
  86.6 2.4 copy.42
  89.6 19.6 %while.38 = (s32[]{:T(128)}, bf16[16,1280]{1,0:T(8,128)(2,1)S(1)}, f32[16,1280]{1,0:T(8,128)S(1)}, f32[16,20]{0,1:T(8,128)}, bf16[512,1280]{0,1:T(8,128)(2,1)}, ...) while((s32[]{:T(128)}, bf16[16,1280]{1,0:T(8,128)(2,1)S(1)}, ...), condition=%wide.region_2.3_spmd.clone, body=%wide.region_0.2_spmd.clone.sunk | while | flops 42620416 | bytes 4643037 | solution.py:153
  89.7 1.5 collective-permute-start
  92.0 1.7 fusion.280
  95.7 1.5 collective-permute-start.2
  97.1 2.3 collective-permute-done.2
  99.5 1.5 collective-permute-start
  101.8 1.7 fusion.280
  105.5 1.5 collective-permute-start.2
  106.9 2.3 collective-permute-done.2
  112.5 56.3 %while.39 = (s32[]{:T(128)}, bf16[16,1280]{1,0:T(8,128)(2,1)}, bf16[16,1280]{1,0:T(8,128)(2,1)}, f32[16,20]{0,1:T(8,128)}, f32[16,20]{0,1:T(8,128)}, /*index=5*/...) while((s32[]{:T(128)}, bf16[16,1280]{1,0:T(8,128)(2,1)}, ...), condition=%wide.region_5.6_spmd.clone, body=%wide.region_4.5_spmd.clone.sunk | while | flops 108647936 | bytes 37869488 | solution.py:185
  113.8 1.5 collective-permute-start.5
  117.9 1.5 collective-permute-start.3
  121.6 1.7 fusion.292
  126.7 1.5 collective-permute-start.7
  128.3 3.1 fusion.294
  131.4 2.1 fusion.295
  133.5 6.1 %bitcast_add_fusion.6 = (f32[512,1280]{0,1:T(8,128)}, f32[512,1280]{0,1:T(8,128)}) fusion(f32[20,512,64]{1,2,0:T(8,128)} %fusion.294, f32[512,1280]{0,1:T(8,128)} %get-tuple-element.528, pred[]{:T(512)S(6)} %compare.3, f32[20,512,64]{1,2,0:T(8,128)} %fusion.295, f32[512,1280]{0,1:T(8,128)} %get-tuple-element.527), kind=kLoop, calls=%fused_computation.11.clone.1 | loop fusion | flops 2621440 | bytes 15728641 | tf_op jit(solution)/shard_map/while/body/eval_jaxpr/add | solution.py:173
  143.5 1.5 collective-permute-start.6
  147.1 1.5 collective-permute-start.4
  149.5 1.7 fusion.292
  155.2 3.1 fusion.294
  158.4 2.1 fusion.295
  160.5 7.7 %bitcast_add_fusion.6 = (f32[512,1280]{0,1:T(8,128)}, f32[512,1280]{0,1:T(8,128)}) fusion(f32[20,512,64]{1,2,0:T(8,128)} %fusion.294, f32[512,1280]{0,1:T(8,128)} %get-tuple-element.528, pred[]{:T(512)S(6)} %compare.3, f32[20,512,64]{1,2,0:T(8,128)} %fusion.295, f32[512,1280]{0,1:T(8,128)} %get-tuple-element.527), kind=kLoop, calls=%fused_computation.11.clone.1 | loop fusion | flops 2621440 | bytes 15728641 | tf_op jit(solution)/shard_map/while/body/eval_jaxpr/add | solution.py:173
  168.8 2.2 multiply_convert_fusion
  172.6 7.7 %fusion.204 = f32[1280,2560]{1,0:T(8,128)} fusion(bf16[512,1280]{1,0:T(8,128)(2,1)S(1)} %copy-done.10, bf16[512,1280]{0,1:T(8,128)(2,1)S(1)} %convert.38, bf16[512,1280]{0,1:T(8,128)(2,1)S(1)} %multiply_convert_fusion), kind=kOutput, calls=%fused_computation.348 | convolution fusion | flops 3360686080 | bytes 17039360 | tf_op jit(solution)/shard_map/dot_general | solution.py:211
  180.6 7.0 %fusion.205 = f32[512,1280]{1,0:T(8,128)S(1)} fusion(bf16[1280,2560]{1,0:T(8,128)(2,1)} %all-gather.2.cloned.1.call-done, bf16[512,1280]{0,1:T(8,128)(2,1)} %copy-done.11, bf16[512,1280]{0,1:T(8,128)(2,1)S(1)} %multiply_convert_fusion), kind=kOutput, calls=%fused_computation.349 | convolution fusion | flops 3360686080 | bytes 11796480 | tf_op jit(solution)/shard_map/dot_general | solution.py:191
  187.7 6.7 %fusion.81 = (f32[1280]{0:T(1024)S(1)}, f32[1280]{0:T(1024)S(1)}, f32[1280]{0:T(1024)S(1)}, f32[1280]{0:T(1024)S(1)}, f32[1280]{0:T(1024)S(1)}, /*index=5*/f32[1...) fusion(bf16[1,527,1280]{2,1,0:T(8,128)(2,1)S(1)} %constant_dyna, ...), kind=kLoop, calls=%fused_computation.195 | loop fusion | flops 37335040 | bytes 27612160 | tf_op jit(solution)/shard_map/reduce_sum | solution.py:199
  194.6 2.6 fusion.52
  197.6 3.3 fusion.61
  202.3 4.6 collective-permute-start.11
  206.9 2.7 stack.127
  210.3 44.2 %psum.22 = f32[1280]{0:T(1024)} all-reduce(f32[1280]{0:T(1024)S(1)} %get-tuple-element.341), channel_id=1, replica_groups=mesh['dp'=16,'ctx'=2] {'dp','ctx'}, use_global_device_ids=true, to_apply=%region_39.40 | all-reduce | flops 1280 | bytes 10240 | tf_op jit(solution)/shard_map/psum | solution.py:209
  254.5 64.0 %reduce-scatter.2.cloned.1.call-done = f32[80,2560]{1,0:T(8,128)} async-done(((f32[1280,2560]{1,0:T(8,128)}), f32[80,2560]{1,0:T(8,128)}) %reduce-scatter.2.cloned.1.call-update) | async-done | bytes 819216 | tf_op jit(solution)/shard_map/reduce_scatter | solution.py:210
  318.8 43.9 %fusion.235 = bf16[1,512,1280]{2,1,0:T(8,128)(2,1)} fusion(f32[512,1280]{1,0:T(8,128)} %copy-done.6, f32[1,512,1280]{2,1,0:T(8,128)} %bitcast.634, f32[1,15,1280]{2,1,0:T(8,128)S(1)} %collective-permute-done.11, f32[1280]{0:T(1024)S(1)} %copy-done.33, f32[1280]{0:T(1024)S(1)} %copy-done.35, f32[1280]{0:T(1024)S(1)} %copy-done.39, f32[1280]{0:T(1024)S(1)} %copy-done.41, ...), kind=kLoop, calls=%fused_computation.396 | loop fusion | flops 60948480 | bytes 9487360 | tf_op jit(solution)/shard_map/broadcast_in_dim | solution.py:208
  362.7 83.9 %all-reduce.3.cloned.1.call-done = f32[31,1280]{1,0:T(8,128)} async-done(((f32[31,1280]{1,0:T(8,128)}), f32[31,1280]{1,0:T(8,128)}) %all-reduce.3.cloned.1.call-update) | async-done | bytes 158736 | tf_op jit(solution)/shard_map/psum | solution.py:209
  446.5 39.3 %all-reduce.5.cloned.1.call-done = f32[80,2560]{1,0:T(8,128)} async-done(((f32[80,2560]{1,0:T(8,128)}), f32[80,2560]{1,0:T(8,128)}) %all-reduce.5.cloned.1.call-update) | async-done | bytes 819216 | tf_op jit(solution)/shard_map/psum | solution.py:218
  485.9 1.6 copy.117
  487.5 2.1 copy.118
  (286 shorter events, 39.0 us)
Async XLA Ops:
  7.2 69.2 %all-gather.2.cloned.1.call-start = ((), (), s32[]{:S(2)}) async-start(), calls=%async_computation.1 | async-start | bytes 6963200 | tf_op jit(solution)/shard_map/all_gather | solution.py:114
  8.7 309.7 %reduce-scatter.2.cloned.1.call-start = ((), (), s32[]{:S(2)}) async-start(), calls=%async_computation.3 | async-start | bytes 13926400 | tf_op jit(solution)/shard_map/reduce_scatter | solution.py:210
  9.6 12.7 %collective-permute-start.8 = (bf16[1,15,1280]{2,1,0:T(8,128)(2,1)S(1)}, bf16[1,15,1280]{2,1,0:T(8,128)(2,1)S(1)}, u32[]{:S(2)}, u32[]{:S(2)}) collective-permute-start(bf16[1,15,1280]{2,1,0:T(8,128)(2,1)S(1)} %get-tuple-element.346), channel_id=1, source_target_pairs={{0,1},{2,3},{4,5},{6,7},{8,9},{10,11},{12,13},{14,15},{16,17},{18,... | collective-permute-start | bytes 115208 | tf_op jit(solution)/shard_map/ppermute | solution.py:14
  14.5 7.8 %collective-permute-start.9 = (bf16[1,15,1280]{2,1,0:T(8,128)(2,1)S(1)}, bf16[1,15,1280]{2,1,0:T(8,128)(2,1)S(1)}, u32[]{:S(2)}, u32[]{:S(2)}) collective-permute-start(bf16[1,15,1280]{2,1,0:T(8,128)(2,1)S(1)} %get-tuple-element.347), channel_id=1, source_target_pairs={{1,0},{3,2},{5,4},{7,6},{9,8},{11,10},{13,12},{15,14},{17,16},{19,... | collective-permute-start | bytes 115208 | tf_op jit(solution)/shard_map/ppermute | solution.py:17
  89.7 9.8 %collective-permute-start = (bf16[16,1280]{1,0:T(8,128)(2,1)S(1)}, bf16[16,1280]{1,0:T(8,128)(2,1)S(1)}, u32[]{:S(2)}, u32[]{:S(2)}) collective-permute-start(bf16[16,1280]{1,0:T(8,128)(2,1)S(1)} %copy.80), channel_id=1, source_target_pairs={{0,1},{1,0},{2,3},{3,2},{4,5},{5,4},{6,7},{7,6},{8,9},{9,8},{10,11... | collective-permute-start | bytes 122888 | tf_op jit(solution)/shard_map/while/body/eval_jaxpr/ppermute | solution.py:25
  94.3 5.1 %collective-permute-start.1 = (f32[16,1280]{1,0:T(8,128)S(1)}, f32[16,1280]{1,0:T(8,128)S(1)}, u32[]{:S(2)}, u32[]{:S(2)}) collective-permute-start(f32[16,1280]{1,0:T(8,128)S(1)} %add.1592), channel_id=1, source_target_pairs={{0,1},{1,0},{2,3},{3,2},{4,5},{5,4},{6,7},{7,6},{8,9},{9,8},{10,11... | collective-permute-start | bytes 245768 | tf_op jit(solution)/shard_map/while/body/eval_jaxpr/ppermute | solution.py:25
  95.7 3.8 collective-permute-start.2
  99.5 9.8 %collective-permute-start = (bf16[16,1280]{1,0:T(8,128)(2,1)S(1)}, bf16[16,1280]{1,0:T(8,128)(2,1)S(1)}, u32[]{:S(2)}, u32[]{:S(2)}) collective-permute-start(bf16[16,1280]{1,0:T(8,128)(2,1)S(1)} %copy.80), channel_id=1, source_target_pairs={{0,1},{1,0},{2,3},{3,2},{4,5},{5,4},{6,7},{7,6},{8,9},{9,8},{10,11... | collective-permute-start | bytes 122888 | tf_op jit(solution)/shard_map/while/body/eval_jaxpr/ppermute | solution.py:25
  104.1 5.1 %collective-permute-start.1 = (f32[16,1280]{1,0:T(8,128)S(1)}, f32[16,1280]{1,0:T(8,128)S(1)}, u32[]{:S(2)}, u32[]{:S(2)}) collective-permute-start(f32[16,1280]{1,0:T(8,128)S(1)} %add.1592), channel_id=1, source_target_pairs={{0,1},{1,0},{2,3},{3,2},{4,5},{5,4},{6,7},{7,6},{8,9},{9,8},{10,11... | collective-permute-start | bytes 245768 | tf_op jit(solution)/shard_map/while/body/eval_jaxpr/ppermute | solution.py:25
  105.5 3.8 collective-permute-start.2
  113.8 25.9 %collective-permute-start.5 = (f32[16,20]{0,1:T(8,128)}, f32[16,20]{0,1:T(8,128)}, u32[]{:S(2)}, u32[]{:S(2)}) collective-permute-start(f32[16,20]{0,1:T(8,128)} %copy.98), channel_id=1, source_target_pairs={{0,1},{1,0},{2,3},{3,2},{4,5},{5,4},{6,7},{7,6},{8,9},{9,8},{10,11... | collective-permute-start | bytes 3848 | tf_op jit(solution)/shard_map/while/body/eval_jaxpr/ppermute | solution.py:25
  116.6 23.1 %collective-permute-start.6 = (f32[16,20]{0,1:T(8,128)}, f32[16,20]{0,1:T(8,128)}, u32[]{:S(2)}, u32[]{:S(2)}) collective-permute-start(f32[16,20]{0,1:T(8,128)} %copy.99), channel_id=1, source_target_pairs={{0,1},{1,0},{2,3},{3,2},{4,5},{5,4},{6,7},{7,6},{8,9},{9,8},{10,11... | collective-permute-start | bytes 3848 | tf_op jit(solution)/shard_map/while/body/eval_jaxpr/ppermute | solution.py:25
  117.9 21.8 %collective-permute-start.3 = (bf16[16,1280]{1,0:T(8,128)(2,1)S(1)}, bf16[16,1280]{1,0:T(8,128)(2,1)}, u32[]{:S(2)}, u32[]{:S(2)}) collective-permute-start(bf16[16,1280]{1,0:T(8,128)(2,1)S(1)} %copy.96), channel_id=1, source_target_pairs={{0,1},{1,0},{2,3},{3,2},{4,5},{5,4},{6,7},{7,6},{8,9},{9,8},{10,11... | collective-permute-start | bytes 122888 | tf_op jit(solution)/shard_map/while/body/eval_jaxpr/ppermute | solution.py:25
  120.2 19.5 %collective-permute-start.4 = (bf16[16,1280]{1,0:T(8,128)(2,1)S(1)}, bf16[16,1280]{1,0:T(8,128)(2,1)}, u32[]{:S(2)}, u32[]{:S(2)}) collective-permute-start(bf16[16,1280]{1,0:T(8,128)(2,1)S(1)} %copy.97), channel_id=1, source_target_pairs={{0,1},{1,0},{2,3},{3,2},{4,5},{5,4},{6,7},{7,6},{8,9},{9,8},{10,11... | collective-permute-start | bytes 122888 | tf_op jit(solution)/shard_map/while/body/eval_jaxpr/ppermute | solution.py:25
  126.7 13.0 %collective-permute-start.7 = (f32[16,1280]{1,0:T(8,128)S(1)}, f32[16,1280]{1,0:T(8,128)S(1)}, u32[]{:S(2)}, u32[]{:S(2)}) collective-permute-start(f32[16,1280]{1,0:T(8,128)S(1)} %add.1597), channel_id=1, source_target_pairs={{0,1},{1,0},{2,3},{3,2},{4,5},{5,4},{6,7},{7,6},{8,9},{9,8},{10,11... | collective-permute-start | bytes 245768 | tf_op jit(solution)/shard_map/while/body/eval_jaxpr/ppermute | solution.py:25
  141.7 26.5 %collective-permute-start.5 = (f32[16,20]{0,1:T(8,128)}, f32[16,20]{0,1:T(8,128)}, u32[]{:S(2)}, u32[]{:S(2)}) collective-permute-start(f32[16,20]{0,1:T(8,128)} %copy.98), channel_id=1, source_target_pairs={{0,1},{1,0},{2,3},{3,2},{4,5},{5,4},{6,7},{7,6},{8,9},{9,8},{10,11... | collective-permute-start | bytes 3848 | tf_op jit(solution)/shard_map/while/body/eval_jaxpr/ppermute | solution.py:25
  143.5 24.6 %collective-permute-start.6 = (f32[16,20]{0,1:T(8,128)}, f32[16,20]{0,1:T(8,128)}, u32[]{:S(2)}, u32[]{:S(2)}) collective-permute-start(f32[16,20]{0,1:T(8,128)} %copy.99), channel_id=1, source_target_pairs={{0,1},{1,0},{2,3},{3,2},{4,5},{5,4},{6,7},{7,6},{8,9},{9,8},{10,11... | collective-permute-start | bytes 3848 | tf_op jit(solution)/shard_map/while/body/eval_jaxpr/ppermute | solution.py:25
  145.8 22.4 %collective-permute-start.3 = (bf16[16,1280]{1,0:T(8,128)(2,1)S(1)}, bf16[16,1280]{1,0:T(8,128)(2,1)}, u32[]{:S(2)}, u32[]{:S(2)}) collective-permute-start(bf16[16,1280]{1,0:T(8,128)(2,1)S(1)} %copy.96), channel_id=1, source_target_pairs={{0,1},{1,0},{2,3},{3,2},{4,5},{5,4},{6,7},{7,6},{8,9},{9,8},{10,11... | collective-permute-start | bytes 122888 | tf_op jit(solution)/shard_map/while/body/eval_jaxpr/ppermute | solution.py:25
  147.1 21.1 %collective-permute-start.4 = (bf16[16,1280]{1,0:T(8,128)(2,1)S(1)}, bf16[16,1280]{1,0:T(8,128)(2,1)}, u32[]{:S(2)}, u32[]{:S(2)}) collective-permute-start(bf16[16,1280]{1,0:T(8,128)(2,1)S(1)} %copy.97), channel_id=1, source_target_pairs={{0,1},{1,0},{2,3},{3,2},{4,5},{5,4},{6,7},{7,6},{8,9},{9,8},{10,11... | collective-permute-start | bytes 122888 | tf_op jit(solution)/shard_map/while/body/eval_jaxpr/ppermute | solution.py:25
  154.6 13.6 %collective-permute-start.7 = (f32[16,1280]{1,0:T(8,128)S(1)}, f32[16,1280]{1,0:T(8,128)S(1)}, u32[]{:S(2)}, u32[]{:S(2)}) collective-permute-start(f32[16,1280]{1,0:T(8,128)S(1)} %add.1597), channel_id=1, source_target_pairs={{0,1},{1,0},{2,3},{3,2},{4,5},{5,4},{6,7},{7,6},{8,9},{9,8},{10,11... | collective-permute-start | bytes 245768 | tf_op jit(solution)/shard_map/while/body/eval_jaxpr/ppermute | solution.py:25
  180.4 266.2 %all-reduce.3.cloned.1.call-start = ((), (), s32[]{:S(2)}) async-start(), calls=%async_computation.2 | async-start | bytes 327680 | tf_op jit(solution)/shard_map/psum | solution.py:209
  197.3 121.2 %copy-start.15 = (f32[1280]{0:T(1024)S(1)}, f32[1280]{0:T(1024)}, u32[]{:S(2)}) copy-start(f32[1280]{0:T(1024)} %copy-done.14) | copy-start | bytes 15364
  197.3 121.2 %copy-start.17 = (f32[1280]{0:T(1024)S(1)}, f32[1280]{0:T(1024)}, u32[]{:S(2)}) copy-start(f32[1280]{0:T(1024)} %copy-done.16) | copy-start | bytes 15364
  197.3 121.2 %copy-start.19 = (f32[1280]{0:T(1024)S(1)}, f32[1280]{0:T(1024)}, u32[]{:S(2)}) copy-start(f32[1280]{0:T(1024)} %copy-done.18) | copy-start | bytes 15364
  197.3 121.2 %copy-start.21 = (f32[1280]{0:T(1024)S(1)}, f32[1280]{0:T(1024)}, u32[]{:S(2)}) copy-start(f32[1280]{0:T(1024)} %copy-done.20) | copy-start | bytes 15364
  197.3 121.2 %copy-start.23 = (f32[1280]{0:T(1024)S(1)}, f32[1280]{0:T(1024)}, u32[]{:S(2)}) copy-start(f32[1280]{0:T(1024)} %copy-done.22) | copy-start | bytes 15364
  197.3 121.2 %copy-start.25 = (f32[1280]{0:T(1024)S(1)}, f32[1280]{0:T(1024)}, u32[]{:S(2)}) copy-start(f32[1280]{0:T(1024)} %copy-done.24) | copy-start | bytes 15364
  197.3 121.2 %copy-start.27 = (f32[1280]{0:T(1024)S(1)}, f32[1280]{0:T(1024)}, u32[]{:S(2)}) copy-start(f32[1280]{0:T(1024)} %copy-done.26) | copy-start | bytes 15364
  197.4 121.2 %copy-start.29 = (f32[1280]{0:T(1024)S(1)}, f32[1280]{0:T(1024)}, u32[]{:S(2)}) copy-start(f32[1280]{0:T(1024)} %copy-done.28) | copy-start | bytes 15364
  197.4 121.2 %copy-start.31 = (f32[1280]{0:T(1024)S(1)}, f32[1280]{0:T(1024)}, u32[]{:S(2)}) copy-start(f32[1280]{0:T(1024)} %copy-done.30) | copy-start | bytes 15364
  197.4 121.2 %copy-start.33 = (f32[1280]{0:T(1024)S(1)}, f32[1280]{0:T(1024)}, u32[]{:S(2)}) copy-start(f32[1280]{0:T(1024)} %copy-done.32) | copy-start | bytes 15364
  197.4 121.2 %copy-start.35 = (f32[1280]{0:T(1024)S(1)}, f32[1280]{0:T(1024)}, u32[]{:S(2)}) copy-start(f32[1280]{0:T(1024)} %copy-done.34) | copy-start | bytes 15364
  197.4 121.2 %copy-start.37 = (f32[1280]{0:T(1024)S(1)}, f32[1280]{0:T(1024)}, u32[]{:S(2)}) copy-start(f32[1280]{0:T(1024)} %copy-done.36) | copy-start | bytes 15364
  197.4 121.2 %copy-start.39 = (f32[1280]{0:T(1024)S(1)}, f32[1280]{0:T(1024)}, u32[]{:S(2)}) copy-start(f32[1280]{0:T(1024)} %copy-done.38) | copy-start | bytes 15364
  197.4 121.2 %copy-start.41 = (f32[1280]{0:T(1024)S(1)}, f32[1280]{0:T(1024)}, u32[]{:S(2)}) copy-start(f32[1280]{0:T(1024)} %copy-done.40) | copy-start | bytes 15364
  197.4 121.2 %copy-start.43 = (f32[1280]{0:T(1024)S(1)}, f32[1280]{0:T(1024)}, u32[]{:S(2)}) copy-start(f32[1280]{0:T(1024)} %copy-done.42) | copy-start | bytes 15364
  197.4 121.2 %copy-start.45 = (f32[1280]{0:T(1024)S(1)}, f32[1280]{0:T(1024)}, u32[]{:S(2)}) copy-start(f32[1280]{0:T(1024)} %copy-done.44) | copy-start | bytes 15364
  197.4 121.2 %copy-start.47 = (f32[1280]{0:T(1024)S(1)}, f32[1280]{0:T(1024)}, u32[]{:S(2)}) copy-start(f32[1280]{0:T(1024)} %copy-done.46) | copy-start | bytes 15364
  197.5 121.2 %copy-start.49 = (f32[1280]{0:T(1024)S(1)}, f32[1280]{0:T(1024)}, u32[]{:S(2)}) copy-start(f32[1280]{0:T(1024)} %copy-done.48) | copy-start | bytes 15364
  197.5 121.2 %copy-start.51 = (f32[1280]{0:T(1024)S(1)}, f32[1280]{0:T(1024)}, u32[]{:S(2)}) copy-start(f32[1280]{0:T(1024)} %copy-done.50) | copy-start | bytes 15364
  197.5 121.2 %copy-start.53 = (f32[1280]{0:T(1024)S(1)}, f32[1280]{0:T(1024)}, u32[]{:S(2)}) copy-start(f32[1280]{0:T(1024)} %copy-done.52) | copy-start | bytes 15364
  197.5 121.2 %copy-start.55 = (f32[1280]{0:T(1024)S(1)}, f32[1280]{0:T(1024)}, u32[]{:S(2)}) copy-start(f32[1280]{0:T(1024)} %copy-done.54) | copy-start | bytes 15364
  197.5 121.2 %copy-start.57 = (f32[1280]{0:T(1024)S(1)}, f32[1280]{0:T(1024)}, u32[]{:S(2)}) copy-start(f32[1280]{0:T(1024)} %copy-done.56) | copy-start | bytes 15364
  197.5 121.2 %copy-start.59 = (f32[1280]{0:T(1024)S(1)}, f32[1280]{0:T(1024)}, u32[]{:S(2)}) copy-start(f32[1280]{0:T(1024)} %copy-done.58) | copy-start | bytes 15364
  197.5 121.2 %copy-start.61 = (f32[1280]{0:T(1024)S(1)}, f32[1280]{0:T(1024)}, u32[]{:S(2)}) copy-start(f32[1280]{0:T(1024)} %copy-done.60) | copy-start | bytes 15364
  201.0 117.5 %collective-permute-start.10 = (f32[1,15,1280]{2,1,0:T(8,128)S(1)}, f32[1,15,1280]{2,1,0:T(8,128)S(1)}, u32[]{:S(2)}, u32[]{:S(2)}) collective-permute-start(f32[1,15,1280]{2,1,0:T(8,128)S(1)} %get-tuple-element.342), channel_id=1, source_target_pairs={{1,0},{3,2},{5,4},{7,6},{9,8},{11,10},{13,12},{15,14},{17,16},{19,... | collective-permute-start | bytes 230408 | tf_op jit(solution)/shard_map/ppermute | solution.py:17
  202.3 116.2 %collective-permute-start.11 = (f32[1,15,1280]{2,1,0:T(8,128)S(1)}, f32[1,15,1280]{2,1,0:T(8,128)S(1)}, u32[]{:S(2)}, u32[]{:S(2)}) collective-permute-start(f32[1,15,1280]{2,1,0:T(8,128)S(1)} %get-tuple-element.343), channel_id=1, source_target_pairs={{0,1},{2,3},{4,5},{6,7},{8,9},{10,11},{12,13},{14,15},{16,17},{18,... | collective-permute-start | bytes 230408 | tf_op jit(solution)/shard_map/ppermute | solution.py:14
  209.6 276.3 %all-reduce.5.cloned.1.call-start = ((), (), s32[]{:S(2)}) async-start(), calls=%async_computation.4 | async-start | bytes 1638400 | tf_op jit(solution)/shard_map/psum | solution.py:218
  (56 other events, 1331.7 us)
Sparse Core Ops, SparseCore 0:
  10.3 66.0 all-gather.1
  180.5 137.9 reduce-scatter.1
  325.5 120.9 all-reduce.2
  448.8 37.0 all-reduce.4
where the time goes:
time: 498 us; the launch traced here: 496 us
  waiting for transfers between devices  233 us (47%)
  other arithmetic  92.3 us (19%)
  blocking collectives  44.2 us (9%)
  matrix products  42.7 us (9%)
  local copies, waits for them, and re-layouts  37.5 us (8%)
  starting transfers between devices  29.8 us (6%)
  between operations  16 us (3%)
    psum x1, waiting for transfers between devices, per_device(): taps_grad, gain_grad = lax.psum((tap_terms, gain_term), ('dp', 'ctx'))  83.9 us
    reduce_scatter x1, waiting for transfers between devices, per_device(): lax.psum_scatter(lax.dot_general(encoded, kv_grad, (((0,), (0,)), ((), ()...  64 us
    psum x1, blocking collectives, per_device(): taps_grad, gain_grad = lax.psum((tap_terms, gain_term), ('dp', 'ctx'))  44.2 us
    broadcast_in_dim x1, other arithmetic, per_device(): frames_grad = (enc_grad + back_conv).astype(jnp.bfloat16)[None]  43.9 us
    all_gather x1, waiting for transfers between devices, per_device(): w_full = lax.all_gather(w_kv, 'dp', axis=0, tiled=True)  41.4 us
    psum x1, waiting for transfers between devices, per_device(): w_kv_grad = lax.psum(data_part, 'ctx')  39.3 us
    ppermute x16, starting transfers between devices, shifted(): return lax.ppermute(value, axis, pairs)  17.5 us
    unnamed x156, local copies, waits for them, and re-layouts  13.9 us
  transfers between devices with their start and end apart: 24, of which 6 were waited for; matrix products, arithmetic and copies ran while one was open for 27% of the time, Pallas kernels for 0%

commit v1 on v0

--- a/solution.py
+++ b/solution.py
@@ -206,7 +206,10 @@
         offset = 2 * rim_width - tap_idx
         back_conv = back_conv + conv_taps[tap_idx] * padded_grad[offset : offset + length]
     frames_grad = (enc_grad + back_conv).astype(jnp.bfloat16)[None]
-    taps_grad, gain_grad = lax.psum((tap_terms, gain_term), ("dp", "ctx"))
+    sites_run = lambda shard_in, axis_tag, dev_axis: lax.psum(
+        lax.psum(shard_in, axis_name=axis_tag), axis_name=dev_axis
+    )
+    taps_grad, gain_grad = sites_run((tap_terms, gain_term), "ctx", "dp")
     data_part = lax.psum_scatter(
         lax.dot_general(
             encoded, kv_grad, (((0,), (0,)), ((), ())), preferred_element_type=jnp.float32

time: 498 us -> 461 us (0.926)
  waiting for transfers between devices: 233 us -> 204 us
  blocking collectives: 44.2 us -> 35.9 us
    psum x2, waiting for transfers between devices: 123 us -> 44.5 us  [the longest x1 44.5 us: per_device(): lax.psum(lax.psum(shard_in, axis_name=axis_tag), axis_name=dev_axis)]
    reduce_scatter x1, waiting for transfers between devices: 64 us -> 114 us  [per_device(): lax.psum_scatter(lax.dot_general(encoded, kv_grad, (((0,), (0,)), ((), ()...]
    psum x1 -> x2, blocking collectives: 44.2 us -> 35.9 us  [the longest x1 30.8 us: per_device(): lax.psum(lax.psum(shard_in, axis_name=axis_tag), axis_name=dev_axis)]
    unnamed x156 -> x158, local copies, waits for them, and re-layouts: 13.9 us -> 12.7 us
  transfers between devices with their start and end apart: 24 -> 24, of which waited for: 6 -> 5; matrix products, arithmetic and copies ran while one was open for 27% -> 29% of each run, Pallas kernels for 0% -> 0%
where the time goes in v1:
time: 461 us; the launch traced here: 459 us
  waiting for transfers between devices  204 us (44%)
  other arithmetic  92.3 us (20%)
  matrix products  42.7 us (9%)
  local copies, waits for them, and re-layouts  37.2 us (8%)
  blocking collectives  35.9 us (8%)
  starting transfers between devices  29.8 us (6%)
  between operations  16 us (3%)
    reduce_scatter x1, waiting for transfers between devices, per_device(): lax.psum_scatter(lax.dot_general(encoded, kv_grad, (((0,), (0,)), ((), ()...  114 us
    psum x1, waiting for transfers between devices, per_device(): lax.psum(lax.psum(shard_in, axis_name=axis_tag), axis_name=dev_axis)  44.5 us
    broadcast_in_dim x1, other arithmetic, per_device(): frames_grad = (enc_grad + back_conv).astype(jnp.bfloat16)[None]  43.9 us
    all_gather x1, waiting for transfers between devices, per_device(): w_full = lax.all_gather(w_kv, 'dp', axis=0, tiled=True)  41.4 us
    psum x1, blocking collectives, per_device(): lax.psum(lax.psum(shard_in, axis_name=axis_tag), axis_name=dev_axis)  30.8 us
    ppermute x16, starting transfers between devices, shifted(): return lax.ppermute(value, axis, pairs)  17.5 us
    add x2, other arithmetic, backward_turn(): value_acc + part_value  13.8 us
    unnamed x158, local copies, waits for them, and re-layouts  12.7 us
  transfers between devices with their start and end apart: 24, of which 5 were waited for; matrix products, arithmetic and copies ran while one was open for 29% of the time, Pallas kernels for 0%

profile of v1, /device:TPU:0, one launch (start us, length us, event | category | flops | bytes accessed | tf_op | source)
XLA Modules:
  0.0 458.6 jit_solution(4511399160331460453)
XLA Ops:
  7.2 1.5 copy.117
  9.6 4.8 %collective-permute-start.8 = (bf16[1,15,1280]{2,1,0:T(8,128)(2,1)S(1)}, bf16[1,15,1280]{2,1,0:T(8,128)(2,1)S(1)}, u32[]{:S(2)}, u32[]{:S(2)}) collective-permute-start(bf16[1,15,1280]{2,1,0:T(8,128)(2,1)S(1)} %get-tuple-element.348), channel_id=1, source_target_pairs={{0,1},{2,3},{4,5},{6,7},{8,9},{10,11},{12,13},{14,15},{16,17},{18,... | collective-permute-start | bytes 115208 | tf_op jit(solution)/shard_map/ppermute | solution.py:14
  16.4 1.5 slice_reduce_fusion.29
  18.0 1.8 slice_reduce_fusion.30
  19.9 1.5 constant_dynamic-update-slice_fusion.1
  22.3 12.4 %fusion.82 = (bf16[512,1280]{1,0:T(8,128)(2,1)}, f32[512,1280]{1,0:T(8,128)}) fusion(bf16[1,512,1280]{2,1,0:T(8,128)(2,1)S(1)} %copy-done.4, f32[1280]{0:T(1024)S(1)} %copy-done.76, bf16[1,527,1280]{2,1,0:T(8,128)(2,1)S(1)} %constant_dynamic-update-slice_fusion, f32[1280]{0:T(1024)S(1)} %get-tuple-element.290, f32[1280]{0:T(1024)S(1)} %get-tuple-element.291, ...), kind=kLoop, calls=%fused_computation.196 | loop fusion | flops 104202240 | bytes 25105920 | tf_op jit(solution)/shard_map/convert_element_type | solution.py:113
  35.0 41.4 %all-gather.2.cloned.1.call-done = bf16[1280,2560]{1,0:T(8,128)(2,1)} async-done(((bf16[80,2560]{1,0:T(8,128)(2,1)}), bf16[1280,2560]{1,0:T(8,128)(2,1)}) %all-gather.2.cloned.1.call-update) | async-done | bytes 6553616 | tf_op jit(solution)/shard_map/all_gather | solution.py:114
  76.4 6.8 %convolution_convert_fusion = bf16[512,2560]{1,0:T(8,128)(2,1)S(1)} fusion(bf16[512,1280]{1,0:T(8,128)(2,1)} %get-tuple-element.337, bf16[1280,2560]{1,0:T(8,128)(2,1)} %all-gather.2.cloned.1.call-done), kind=kOutput, calls=%fused_computation.72 | convolution fusion | flops 3356753920 | bytes 10485760 | tf_op jit(solution)/shard_map/dot_general | solution.py:115
  83.3 1.7 fusion.242
  85.0 1.6 copy.43
  86.6 2.4 copy.42
  89.6 19.6 %while.38 = (s32[]{:T(128)}, bf16[16,1280]{1,0:T(8,128)(2,1)S(1)}, f32[16,1280]{1,0:T(8,128)S(1)}, f32[16,20]{0,1:T(8,128)}, bf16[512,1280]{0,1:T(8,128)(2,1)}, ...) while((s32[]{:T(128)}, bf16[16,1280]{1,0:T(8,128)(2,1)S(1)}, ...), condition=%wide.region_2.3_spmd.clone, body=%wide.region_0.2_spmd.clone.sunk | while | flops 42620416 | bytes 4643037 | solution.py:153
  89.7 1.5 collective-permute-start
  92.0 1.7 fusion.280
  95.7 1.5 collective-permute-start.2
  97.1 2.3 collective-permute-done.2
  99.5 1.5 collective-permute-start
  101.8 1.7 fusion.280
  105.5 1.5 collective-permute-start.2
  106.9 2.3 collective-permute-done.2
  112.5 56.3 %while.39 = (s32[]{:T(128)}, bf16[16,1280]{1,0:T(8,128)(2,1)}, bf16[16,1280]{1,0:T(8,128)(2,1)}, f32[16,20]{0,1:T(8,128)}, f32[16,20]{0,1:T(8,128)}, /*index=5*/...) while((s32[]{:T(128)}, bf16[16,1280]{1,0:T(8,128)(2,1)}, ...), condition=%wide.region_5.6_spmd.clone, body=%wide.region_4.5_spmd.clone.sunk | while | flops 108647936 | bytes 37869488 | solution.py:185
  113.8 1.5 collective-permute-start.5
  117.9 1.5 collective-permute-start.3
  121.6 1.7 fusion.292
  126.7 1.5 collective-permute-start.7
  128.3 3.1 fusion.294
  131.4 2.1 fusion.295
  133.5 6.1 %bitcast_add_fusion.6 = (f32[512,1280]{0,1:T(8,128)}, f32[512,1280]{0,1:T(8,128)}) fusion(f32[20,512,64]{1,2,0:T(8,128)} %fusion.294, f32[512,1280]{0,1:T(8,128)} %get-tuple-element.530, pred[]{:T(512)S(6)} %compare.3, f32[20,512,64]{1,2,0:T(8,128)} %fusion.295, f32[512,1280]{0,1:T(8,128)} %get-tuple-element.529), kind=kLoop, calls=%fused_computation.11.clone.1 | loop fusion | flops 2621440 | bytes 15728641 | tf_op jit(solution)/shard_map/while/body/eval_jaxpr/add | solution.py:173
  143.5 1.5 collective-permute-start.6
  147.1 1.5 collective-permute-start.4
  149.5 1.7 fusion.292
  155.2 3.1 fusion.294
  158.4 2.1 fusion.295
  160.5 7.7 %bitcast_add_fusion.6 = (f32[512,1280]{0,1:T(8,128)}, f32[512,1280]{0,1:T(8,128)}) fusion(f32[20,512,64]{1,2,0:T(8,128)} %fusion.294, f32[512,1280]{0,1:T(8,128)} %get-tuple-element.530, pred[]{:T(512)S(6)} %compare.3, f32[20,512,64]{1,2,0:T(8,128)} %fusion.295, f32[512,1280]{0,1:T(8,128)} %get-tuple-element.529), kind=kLoop, calls=%fused_computation.11.clone.1 | loop fusion | flops 2621440 | bytes 15728641 | tf_op jit(solution)/shard_map/while/body/eval_jaxpr/add | solution.py:173
  168.8 2.2 multiply_convert_fusion
  172.6 7.7 %fusion.204 = f32[1280,2560]{1,0:T(8,128)} fusion(bf16[512,1280]{1,0:T(8,128)(2,1)S(1)} %copy-done.10, bf16[512,1280]{0,1:T(8,128)(2,1)S(1)} %convert.38, bf16[512,1280]{0,1:T(8,128)(2,1)S(1)} %multiply_convert_fusion), kind=kOutput, calls=%fused_computation.348 | convolution fusion | flops 3360686080 | bytes 17039360 | tf_op jit(solution)/shard_map/dot_general | solution.py:214
  180.6 7.0 %fusion.205 = f32[512,1280]{1,0:T(8,128)S(1)} fusion(bf16[1280,2560]{1,0:T(8,128)(2,1)} %all-gather.2.cloned.1.call-done, bf16[512,1280]{0,1:T(8,128)(2,1)} %copy-done.11, bf16[512,1280]{0,1:T(8,128)(2,1)S(1)} %multiply_convert_fusion), kind=kOutput, calls=%fused_computation.349 | convolution fusion | flops 3360686080 | bytes 11796480 | tf_op jit(solution)/shard_map/dot_general | solution.py:191
  187.7 6.7 %fusion.81 = (f32[1280]{0:T(1024)S(1)}, f32[1280]{0:T(1024)S(1)}, f32[1280]{0:T(1024)S(1)}, f32[1280]{0:T(1024)S(1)}, f32[1280]{0:T(1024)S(1)}, /*index=5*/f32[1...) fusion(bf16[1,527,1280]{2,1,0:T(8,128)(2,1)S(1)} %constant_dyna, ...), kind=kLoop, calls=%fused_computation.195 | loop fusion | flops 37335040 | bytes 27612160 | tf_op jit(solution)/shard_map/reduce_sum | solution.py:199
  194.6 2.6 fusion.52
  197.6 3.3 fusion.61
  201.0 2.7 stack.127
  203.7 113.8 %reduce-scatter.2.cloned.1.call-done = f32[80,2560]{1,0:T(8,128)} async-done(((f32[1280,2560]{1,0:T(8,128)}), f32[80,2560]{1,0:T(8,128)}) %reduce-scatter.2.cloned.1.call-update) | async-done | bytes 819216 | tf_op jit(solution)/shard_map/reduce_scatter | solution.py:213
  319.8 4.6 collective-permute-start.11
  325.0 5.1 %psum.37 = f32[1280]{0:T(1024)S(1)} all-reduce(f32[1280]{0:T(1024)S(1)} %get-tuple-element.343), channel_id=1, replica_groups=mesh['dp'=16,'ctx'=2] {'ctx'}, use_global_device_ids=true, to_apply=%region_40.41 | all-reduce | flops 1280 | bytes 10240 | tf_op jit(solution)/shard_map/psum | solution.py:210
  330.1 30.8 %psum.38 = f32[1280]{0:T(1024)} all-reduce(f32[1280]{0:T(1024)S(1)} %psum.37), channel_id=1, replica_groups=mesh['dp'=16,'ctx'=2] {'dp'}, use_global_device_ids=true, to_apply=%region_41.42 | all-reduce | flops 1280 | bytes 10240 | tf_op jit(solution)/shard_map/psum | solution.py:209
  361.2 43.9 %fusion.235 = bf16[1,512,1280]{2,1,0:T(8,128)(2,1)} fusion(f32[512,1280]{1,0:T(8,128)} %copy-done.6, f32[1,512,1280]{2,1,0:T(8,128)} %bitcast.634, f32[1,15,1280]{2,1,0:T(8,128)S(1)} %collective-permute-done.11, f32[1280]{0:T(1024)S(1)} %copy-done.34, f32[1280]{0:T(1024)S(1)} %copy-done.36, f32[1280]{0:T(1024)S(1)} %copy-done.40, f32[1280]{0:T(1024)S(1)} %copy-done.42, ...), kind=kLoop, calls=%fused_computation.396 | loop fusion | flops 60948480 | bytes 9487360 | tf_op jit(solution)/shard_map/broadcast_in_dim | solution.py:208
  405.1 44.5 %all-reduce.4.cloned.1.call-done = f32[31,1280]{1,0:T(8,128)} async-done(((f32[31,1280]{1,0:T(8,128)}), f32[31,1280]{1,0:T(8,128)}) %all-reduce.4.cloned.1.call-update) | async-done | bytes 158736 | tf_op jit(solution)/shard_map/psum | solution.py:209
  449.6 1.6 copy.118
  (289 shorter events, 39.3 us)
Async XLA Ops:
  7.2 69.2 %all-gather.2.cloned.1.call-start = ((), (), s32[]{:S(2)}) async-start(), calls=%async_computation.1 | async-start | bytes 6963200 | tf_op jit(solution)/shard_map/all_gather | solution.py:114
  8.7 308.7 %reduce-scatter.2.cloned.1.call-start = ((), (), s32[]{:S(2)}) async-start(), calls=%async_computation.3 | async-start | bytes 13926400 | tf_op jit(solution)/shard_map/reduce_scatter | solution.py:213
  9.6 12.7 %collective-permute-start.8 = (bf16[1,15,1280]{2,1,0:T(8,128)(2,1)S(1)}, bf16[1,15,1280]{2,1,0:T(8,128)(2,1)S(1)}, u32[]{:S(2)}, u32[]{:S(2)}) collective-permute-start(bf16[1,15,1280]{2,1,0:T(8,128)(2,1)S(1)} %get-tuple-element.348), channel_id=1, source_target_pairs={{0,1},{2,3},{4,5},{6,7},{8,9},{10,11},{12,13},{14,15},{16,17},{18,... | collective-permute-start | bytes 115208 | tf_op jit(solution)/shard_map/ppermute | solution.py:14
  14.5 7.8 %collective-permute-start.9 = (bf16[1,15,1280]{2,1,0:T(8,128)(2,1)S(1)}, bf16[1,15,1280]{2,1,0:T(8,128)(2,1)S(1)}, u32[]{:S(2)}, u32[]{:S(2)}) collective-permute-start(bf16[1,15,1280]{2,1,0:T(8,128)(2,1)S(1)} %get-tuple-element.349), channel_id=1, source_target_pairs={{1,0},{3,2},{5,4},{7,6},{9,8},{11,10},{13,12},{15,14},{17,16},{19,... | collective-permute-start | bytes 115208 | tf_op jit(solution)/shard_map/ppermute | solution.py:17
  89.7 9.8 %collective-permute-start = (bf16[16,1280]{1,0:T(8,128)(2,1)S(1)}, bf16[16,1280]{1,0:T(8,128)(2,1)S(1)}, u32[]{:S(2)}, u32[]{:S(2)}) collective-permute-start(bf16[16,1280]{1,0:T(8,128)(2,1)S(1)} %copy.80), channel_id=1, source_target_pairs={{0,1},{1,0},{2,3},{3,2},{4,5},{5,4},{6,7},{7,6},{8,9},{9,8},{10,11... | collective-permute-start | bytes 122888 | tf_op jit(solution)/shard_map/while/body/eval_jaxpr/ppermute | solution.py:25
  94.3 5.1 %collective-permute-start.1 = (f32[16,1280]{1,0:T(8,128)S(1)}, f32[16,1280]{1,0:T(8,128)S(1)}, u32[]{:S(2)}, u32[]{:S(2)}) collective-permute-start(f32[16,1280]{1,0:T(8,128)S(1)} %add.1596), channel_id=1, source_target_pairs={{0,1},{1,0},{2,3},{3,2},{4,5},{5,4},{6,7},{7,6},{8,9},{9,8},{10,11... | collective-permute-start | bytes 245768 | tf_op jit(solution)/shard_map/while/body/eval_jaxpr/ppermute | solution.py:25
  95.7 3.8 collective-permute-start.2
  99.5 9.8 %collective-permute-start = (bf16[16,1280]{1,0:T(8,128)(2,1)S(1)}, bf16[16,1280]{1,0:T(8,128)(2,1)S(1)}, u32[]{:S(2)}, u32[]{:S(2)}) collective-permute-start(bf16[16,1280]{1,0:T(8,128)(2,1)S(1)} %copy.80), channel_id=1, source_target_pairs={{0,1},{1,0},{2,3},{3,2},{4,5},{5,4},{6,7},{7,6},{8,9},{9,8},{10,11... | collective-permute-start | bytes 122888 | tf_op jit(solution)/shard_map/while/body/eval_jaxpr/ppermute | solution.py:25
  104.1 5.1 %collective-permute-start.1 = (f32[16,1280]{1,0:T(8,128)S(1)}, f32[16,1280]{1,0:T(8,128)S(1)}, u32[]{:S(2)}, u32[]{:S(2)}) collective-permute-start(f32[16,1280]{1,0:T(8,128)S(1)} %add.1596), channel_id=1, source_target_pairs={{0,1},{1,0},{2,3},{3,2},{4,5},{5,4},{6,7},{7,6},{8,9},{9,8},{10,11... | collective-permute-start | bytes 245768 | tf_op jit(solution)/shard_map/while/body/eval_jaxpr/ppermute | solution.py:25
  105.5 3.8 collective-permute-start.2
  113.8 25.9 %collective-permute-start.5 = (f32[16,20]{0,1:T(8,128)}, f32[16,20]{0,1:T(8,128)}, u32[]{:S(2)}, u32[]{:S(2)}) collective-permute-start(f32[16,20]{0,1:T(8,128)} %copy.98), channel_id=1, source_target_pairs={{0,1},{1,0},{2,3},{3,2},{4,5},{5,4},{6,7},{7,6},{8,9},{9,8},{10,11... | collective-permute-start | bytes 3848 | tf_op jit(solution)/shard_map/while/body/eval_jaxpr/ppermute | solution.py:25
  116.6 23.1 %collective-permute-start.6 = (f32[16,20]{0,1:T(8,128)}, f32[16,20]{0,1:T(8,128)}, u32[]{:S(2)}, u32[]{:S(2)}) collective-permute-start(f32[16,20]{0,1:T(8,128)} %copy.99), channel_id=1, source_target_pairs={{0,1},{1,0},{2,3},{3,2},{4,5},{5,4},{6,7},{7,6},{8,9},{9,8},{10,11... | collective-permute-start | bytes 3848 | tf_op jit(solution)/shard_map/while/body/eval_jaxpr/ppermute | solution.py:25
  117.9 21.8 %collective-permute-start.3 = (bf16[16,1280]{1,0:T(8,128)(2,1)S(1)}, bf16[16,1280]{1,0:T(8,128)(2,1)}, u32[]{:S(2)}, u32[]{:S(2)}) collective-permute-start(bf16[16,1280]{1,0:T(8,128)(2,1)S(1)} %copy.96), channel_id=1, source_target_pairs={{0,1},{1,0},{2,3},{3,2},{4,5},{5,4},{6,7},{7,6},{8,9},{9,8},{10,11... | collective-permute-start | bytes 122888 | tf_op jit(solution)/shard_map/while/body/eval_jaxpr/ppermute | solution.py:25
  120.2 19.5 %collective-permute-start.4 = (bf16[16,1280]{1,0:T(8,128)(2,1)S(1)}, bf16[16,1280]{1,0:T(8,128)(2,1)}, u32[]{:S(2)}, u32[]{:S(2)}) collective-permute-start(bf16[16,1280]{1,0:T(8,128)(2,1)S(1)} %copy.97), channel_id=1, source_target_pairs={{0,1},{1,0},{2,3},{3,2},{4,5},{5,4},{6,7},{7,6},{8,9},{9,8},{10,11... | collective-permute-start | bytes 122888 | tf_op jit(solution)/shard_map/while/body/eval_jaxpr/ppermute | solution.py:25
  126.7 13.0 %collective-permute-start.7 = (f32[16,1280]{1,0:T(8,128)S(1)}, f32[16,1280]{1,0:T(8,128)S(1)}, u32[]{:S(2)}, u32[]{:S(2)}) collective-permute-start(f32[16,1280]{1,0:T(8,128)S(1)} %add.1601), channel_id=1, source_target_pairs={{0,1},{1,0},{2,3},{3,2},{4,5},{5,4},{6,7},{7,6},{8,9},{9,8},{10,11... | collective-permute-start | bytes 245768 | tf_op jit(solution)/shard_map/while/body/eval_jaxpr/ppermute | solution.py:25
  141.7 26.5 %collective-permute-start.5 = (f32[16,20]{0,1:T(8,128)}, f32[16,20]{0,1:T(8,128)}, u32[]{:S(2)}, u32[]{:S(2)}) collective-permute-start(f32[16,20]{0,1:T(8,128)} %copy.98), channel_id=1, source_target_pairs={{0,1},{1,0},{2,3},{3,2},{4,5},{5,4},{6,7},{7,6},{8,9},{9,8},{10,11... | collective-permute-start | bytes 3848 | tf_op jit(solution)/shard_map/while/body/eval_jaxpr/ppermute | solution.py:25
  143.5 24.6 %collective-permute-start.6 = (f32[16,20]{0,1:T(8,128)}, f32[16,20]{0,1:T(8,128)}, u32[]{:S(2)}, u32[]{:S(2)}) collective-permute-start(f32[16,20]{0,1:T(8,128)} %copy.99), channel_id=1, source_target_pairs={{0,1},{1,0},{2,3},{3,2},{4,5},{5,4},{6,7},{7,6},{8,9},{9,8},{10,11... | collective-permute-start | bytes 3848 | tf_op jit(solution)/shard_map/while/body/eval_jaxpr/ppermute | solution.py:25
  145.8 22.4 %collective-permute-start.3 = (bf16[16,1280]{1,0:T(8,128)(2,1)S(1)}, bf16[16,1280]{1,0:T(8,128)(2,1)}, u32[]{:S(2)}, u32[]{:S(2)}) collective-permute-start(bf16[16,1280]{1,0:T(8,128)(2,1)S(1)} %copy.96), channel_id=1, source_target_pairs={{0,1},{1,0},{2,3},{3,2},{4,5},{5,4},{6,7},{7,6},{8,9},{9,8},{10,11... | collective-permute-start | bytes 122888 | tf_op jit(solution)/shard_map/while/body/eval_jaxpr/ppermute | solution.py:25
  147.1 21.1 %collective-permute-start.4 = (bf16[16,1280]{1,0:T(8,128)(2,1)S(1)}, bf16[16,1280]{1,0:T(8,128)(2,1)}, u32[]{:S(2)}, u32[]{:S(2)}) collective-permute-start(bf16[16,1280]{1,0:T(8,128)(2,1)S(1)} %copy.97), channel_id=1, source_target_pairs={{0,1},{1,0},{2,3},{3,2},{4,5},{5,4},{6,7},{7,6},{8,9},{9,8},{10,11... | collective-permute-start | bytes 122888 | tf_op jit(solution)/shard_map/while/body/eval_jaxpr/ppermute | solution.py:25
  154.6 13.6 %collective-permute-start.7 = (f32[16,1280]{1,0:T(8,128)S(1)}, f32[16,1280]{1,0:T(8,128)S(1)}, u32[]{:S(2)}, u32[]{:S(2)}) collective-permute-start(f32[16,1280]{1,0:T(8,128)S(1)} %add.1601), channel_id=1, source_target_pairs={{0,1},{1,0},{2,3},{3,2},{4,5},{5,4},{6,7},{7,6},{8,9},{9,8},{10,11... | collective-permute-start | bytes 245768 | tf_op jit(solution)/shard_map/while/body/eval_jaxpr/ppermute | solution.py:25
  180.4 180.5 %all-reduce.6.cloned.1.call-start = ((), (), s32[]{:S(2)}) async-start(), calls=%async_computation.4 | async-start | bytes 1966080 | tf_op jit(solution)/shard_map/psum | solution.py:210
  197.3 163.6 %copy-start.16 = (f32[1280]{0:T(1024)S(1)}, f32[1280]{0:T(1024)}, u32[]{:S(2)}) copy-start(f32[1280]{0:T(1024)} %copy-done.15) | copy-start | bytes 15364
  197.3 163.6 %copy-start.18 = (f32[1280]{0:T(1024)S(1)}, f32[1280]{0:T(1024)}, u32[]{:S(2)}) copy-start(f32[1280]{0:T(1024)} %copy-done.17) | copy-start | bytes 15364
  197.3 163.6 %copy-start.20 = (f32[1280]{0:T(1024)S(1)}, f32[1280]{0:T(1024)}, u32[]{:S(2)}) copy-start(f32[1280]{0:T(1024)} %copy-done.19) | copy-start | bytes 15364
  197.3 163.6 %copy-start.22 = (f32[1280]{0:T(1024)S(1)}, f32[1280]{0:T(1024)}, u32[]{:S(2)}) copy-start(f32[1280]{0:T(1024)} %copy-done.21) | copy-start | bytes 15364
  197.3 163.6 %copy-start.24 = (f32[1280]{0:T(1024)S(1)}, f32[1280]{0:T(1024)}, u32[]{:S(2)}) copy-start(f32[1280]{0:T(1024)} %copy-done.23) | copy-start | bytes 15364
  197.3 163.6 %copy-start.26 = (f32[1280]{0:T(1024)S(1)}, f32[1280]{0:T(1024)}, u32[]{:S(2)}) copy-start(f32[1280]{0:T(1024)} %copy-done.25) | copy-start | bytes 15364
  197.3 163.6 %copy-start.28 = (f32[1280]{0:T(1024)S(1)}, f32[1280]{0:T(1024)}, u32[]{:S(2)}) copy-start(f32[1280]{0:T(1024)} %copy-done.27) | copy-start | bytes 15364
  197.3 163.6 %copy-start.30 = (f32[1280]{0:T(1024)S(1)}, f32[1280]{0:T(1024)}, u32[]{:S(2)}) copy-start(f32[1280]{0:T(1024)} %copy-done.29) | copy-start | bytes 15364
  197.4 163.6 %copy-start.32 = (f32[1280]{0:T(1024)S(1)}, f32[1280]{0:T(1024)}, u32[]{:S(2)}) copy-start(f32[1280]{0:T(1024)} %copy-done.31) | copy-start | bytes 15364
  197.4 163.6 %copy-start.34 = (f32[1280]{0:T(1024)S(1)}, f32[1280]{0:T(1024)}, u32[]{:S(2)}) copy-start(f32[1280]{0:T(1024)} %copy-done.33) | copy-start | bytes 15364
  197.4 163.6 %copy-start.36 = (f32[1280]{0:T(1024)S(1)}, f32[1280]{0:T(1024)}, u32[]{:S(2)}) copy-start(f32[1280]{0:T(1024)} %copy-done.35) | copy-start | bytes 15364
  197.4 163.6 %copy-start.38 = (f32[1280]{0:T(1024)S(1)}, f32[1280]{0:T(1024)}, u32[]{:S(2)}) copy-start(f32[1280]{0:T(1024)} %copy-done.37) | copy-start | bytes 15364
  197.4 163.6 %copy-start.40 = (f32[1280]{0:T(1024)S(1)}, f32[1280]{0:T(1024)}, u32[]{:S(2)}) copy-start(f32[1280]{0:T(1024)} %copy-done.39) | copy-start | bytes 15364
  197.4 163.6 %copy-start.42 = (f32[1280]{0:T(1024)S(1)}, f32[1280]{0:T(1024)}, u32[]{:S(2)}) copy-start(f32[1280]{0:T(1024)} %copy-done.41) | copy-start | bytes 15364
  197.4 163.6 %copy-start.44 = (f32[1280]{0:T(1024)S(1)}, f32[1280]{0:T(1024)}, u32[]{:S(2)}) copy-start(f32[1280]{0:T(1024)} %copy-done.43) | copy-start | bytes 15364
  197.4 163.6 %copy-start.46 = (f32[1280]{0:T(1024)S(1)}, f32[1280]{0:T(1024)}, u32[]{:S(2)}) copy-start(f32[1280]{0:T(1024)} %copy-done.45) | copy-start | bytes 15364
  197.4 163.6 %copy-start.48 = (f32[1280]{0:T(1024)S(1)}, f32[1280]{0:T(1024)}, u32[]{:S(2)}) copy-start(f32[1280]{0:T(1024)} %copy-done.47) | copy-start | bytes 15364
  197.4 163.6 %copy-start.50 = (f32[1280]{0:T(1024)S(1)}, f32[1280]{0:T(1024)}, u32[]{:S(2)}) copy-start(f32[1280]{0:T(1024)} %copy-done.49) | copy-start | bytes 15364
  197.5 163.6 %copy-start.52 = (f32[1280]{0:T(1024)S(1)}, f32[1280]{0:T(1024)}, u32[]{:S(2)}) copy-start(f32[1280]{0:T(1024)} %copy-done.51) | copy-start | bytes 15364
  197.5 163.6 %copy-start.54 = (f32[1280]{0:T(1024)S(1)}, f32[1280]{0:T(1024)}, u32[]{:S(2)}) copy-start(f32[1280]{0:T(1024)} %copy-done.53) | copy-start | bytes 15364
  197.5 163.6 %copy-start.56 = (f32[1280]{0:T(1024)S(1)}, f32[1280]{0:T(1024)}, u32[]{:S(2)}) copy-start(f32[1280]{0:T(1024)} %copy-done.55) | copy-start | bytes 15364
  197.5 163.6 %copy-start.58 = (f32[1280]{0:T(1024)S(1)}, f32[1280]{0:T(1024)}, u32[]{:S(2)}) copy-start(f32[1280]{0:T(1024)} %copy-done.57) | copy-start | bytes 15364
  197.5 163.6 %copy-start.60 = (f32[1280]{0:T(1024)S(1)}, f32[1280]{0:T(1024)}, u32[]{:S(2)}) copy-start(f32[1280]{0:T(1024)} %copy-done.59) | copy-start | bytes 15364
  197.5 163.6 %copy-start.62 = (f32[1280]{0:T(1024)S(1)}, f32[1280]{0:T(1024)}, u32[]{:S(2)}) copy-start(f32[1280]{0:T(1024)} %copy-done.61) | copy-start | bytes 15364
  317.5 132.1 %all-reduce.4.cloned.1.call-start = ((), (), s32[]{:S(2)}) async-start(), calls=%async_computation.2 | async-start | bytes 327680 | tf_op jit(solution)/shard_map/psum | solution.py:209
  318.5 42.4 %collective-permute-start.10 = (f32[1,15,1280]{2,1,0:T(8,128)S(1)}, f32[1,15,1280]{2,1,0:T(8,128)S(1)}, u32[]{:S(2)}, u32[]{:S(2)}) collective-permute-start(f32[1,15,1280]{2,1,0:T(8,128)S(1)} %get-tuple-element.344), channel_id=1, source_target_pairs={{1,0},{3,2},{5,4},{7,6},{9,8},{11,10},{13,12},{15,14},{17,16},{19,... | collective-permute-start | bytes 230408 | tf_op jit(solution)/shard_map/ppermute | solution.py:17
  319.8 41.1 %collective-permute-start.11 = (f32[1,15,1280]{2,1,0:T(8,128)S(1)}, f32[1,15,1280]{2,1,0:T(8,128)S(1)}, u32[]{:S(2)}, u32[]{:S(2)}) collective-permute-start(f32[1,15,1280]{2,1,0:T(8,128)S(1)} %get-tuple-element.345), channel_id=1, source_target_pairs={{0,1},{2,3},{4,5},{6,7},{8,9},{10,11},{12,13},{14,15},{16,17},{18,... | collective-permute-start | bytes 230408 | tf_op jit(solution)/shard_map/ppermute | solution.py:14
  (57 other events, 1790.8 us)
Sparse Core Ops, SparseCore 0:
  10.3 66.0 all-gather.1
  180.5 136.9 reduce-scatter.1
  320.5 37.9 all-reduce.5
  361.8 87.7 all-reduce.3
